TPU v7x, 128 devices: a whole 4x4x4 slice. The times are simulated.
128 devices in a mesh: row: 8 (over x, core), ch: 16 (over y, z).
Axes of the slice: x: 4, y: 4, z: 4, core: 2. Of those that a mesh axis runs over, the one named last changes fastest.
Arguments:
- surface_rows: float32 [4, 8, 896, 1024], P(None, None, 'ch', 'row'), may hold values from -6 to 6
- he_states: float32 [256, 1024], P(None, 'row'), may hold values from -0.1875 to 0.1875
- energies: float32 [256], replicated, may hold values from -2 to 2
- state_phase: float32 [256], replicated, may hold values from -3.140625 to 3.140625
- momentum_phase: float32 [256], replicated, may hold values from -3.140625 to 3.140625
- bessel_value: float32 [32, 256], replicated, may hold values from -6 to 6
- bessel_slope: float32 [32, 256], replicated, may hold values from -6 to 6
- channel_l2: int32 [896], replicated, may hold values from 0 to 31
- surface_list: int32 [896], P('ch'), may hold values from 0 to 895, each once
- previous: float32 [896, 256, 2, 256], P(None, ('row', 'ch')), may hold values from -6 to 6
- coupling: float32 [2048, 896], replicated, may hold values from -0.1875 to 0.1875
Outputs:
- amplitudes: float32 [896, 256, 2, 256], P(None, ('row', 'ch'))
- spectrum: float32 [2048, 256, 2, 256], P(None, ('row', 'ch'))
Inputs may be any that keep to these rules, and one draw needn't show every extreme that they name: `surface_list`: each channel number appears exactly once.
All inputs are finite; a program needn't handle non-finite values.
Results may differ from a plain program's by a relative error of at most 0.0001.
Values sent between devices are 32-bit elements; how exact they have to be, the bound alone decides.
A program may use at most 128 MiB of HBM per device.

v0:
```python
import functools
import jax, jax.numpy as jnp
from jax import lax
from jax.experimental import pallas as pl
from jax.experimental.pallas import tpu as pltpu
from jax.sharding import PartitionSpec as P

f32, bf16, i32 = jnp.float32, jnp.bfloat16, jnp.int32
time_step, momentum_top = 0.4, 2.0
NCH, NG = 896, 2048
ANY = pl.BlockSpec(memory_space=pl.ANY)
VM = pl.BlockSpec(memory_space=pltpu.VMEM)
SM = pl.BlockSpec(memory_space=pltpu.SMEM)

def split2(x):
    hi = x.astype(bf16).astype(f32)
    return hi, x - hi

def dot(a, b):
    return lax.dot_general(a, b, (((1,), (0,)), ((), ())), preferred_element_type=f32)

MESH = pl.DeviceIdType.MESH
NT = (((1,), (1,)), ((), ()))
HALF = 896


def exchange_kernel(surf_hbm, he_ref, own_list, z_ref, l_ref,
                    own_s, other, own, got, rel, fromx, ybuf,
                    load_sem, core_send, core_recv, rel_send, rel_recv,
                    dir_send, dir_recv, comb_send, comb_recv,
                    out_send, out_recv, list_send, list_recv):
    row, ch = lax.axis_index("row"), lax.axis_index("ch")
    x, core = row // 2, row % 2
    right, left, across = (x + 1) % 4, (x + 3) % 4, (x + 2) % 4
    partner = {"row": 2 * x + 1 - core}
    to_right, to_left = {"row": 2 * right + core}, {"row": 2 * left + core}

    load = pltpu.make_async_copy(surf_hbm, own_s, load_sem)
    load.start()
    barrier = pltpu.get_barrier_semaphore()
    for target in (partner, to_right, to_left):
        pl.semaphore_signal(barrier, inc=1, device_id=target, device_id_type=MESH)
    for d in range(1, 16):
        pl.semaphore_signal(barrier, inc=1, device_id={"ch": (ch + d) % 16}, device_id_type=MESH)

    parts = []
    for side in (1 - core, core):
        for n in range(2):
            for xx in range(4):
                parts.append(he_ref[xx, side, pl.ds(n, 16, stride=2), :])
    he = jnp.concatenate(parts, axis=0)
    h_hi, h_lo = split2(he)
    h_left = jnp.concatenate([h_hi, h_hi, h_lo], axis=1).astype(bf16)
    for n in range(2):
        for tail in (14, 15):
            ybuf[n, pl.ds(tail, 16, stride=16), :] = jnp.zeros((16, 128), f32)
    load.wait()
    for jc in range(7):
        rows = jnp.concatenate([own_s[pl.ds(jc * 8 + j, 32, stride=56), :] for j in range(8)], axis=0)
        s_hi, s_lo = split2(rows)
        s_right = jnp.concatenate([s_hi, s_lo, s_hi], axis=1).astype(bf16)
        part = lax.dot_general(h_left, s_right, NT, preferred_element_type=f32)
        lanes = slice(jc * 256, (jc + 1) * 256)
        for n in range(2):
            for xx in range(4):
                at = (n * 4 + xx) * 16
                other[n, xx, :, lanes] = part[at:at + 16]
                own[n, xx, :, lanes] = part[128 + at:144 + at]
    pl.semaphore_wait(barrier, 18)

    def remote(src, dst, send, recv, target):
        return pltpu.make_async_remote_copy(src_ref=src, dst_ref=dst, send_sem=send, recv_sem=recv,
                                            device_id=target, device_id_type=MESH)

    core_copies = [remote(other.at[n], got.at[n], core_send.at[n], core_recv.at[n], partner) for n in range(2)]
    for copy in core_copies:
        copy.start()
    here = pl.ds(pl.multiple_of(ch * 16, 16), 16)
    list_copies = [remote(own_list, l_ref.at[here], list_send.at[d], list_recv.at[d], {"ch": (ch + d) % 16})
                   for d in range(1, 16)]
    for copy in list_copies:
        copy.start()
    l_ref[here] = own_list[...]

    halves = (pl.ds(0, HALF), pl.ds(HALF, HALF))
    relays, directs, combs, outs = [], [], [], []
    for n in range(2):
        core_copies[n].wait()
        for h, target in ((0, to_right), (1, to_left)):
            own[n, across, :, halves[h]] += got[n, across, :, halves[h]]
            relays.append(remote(own.at[n, across, :, halves[h]], rel.at[n, h], rel_send.at[n, h],
                                 rel_recv.at[n, h], target))
            relays[-1].start()
        for h, target, block in ((1, to_right, right), (0, to_left, left)):
            own[n, block, :, halves[h]] += got[n, block, :, halves[h]]
            directs.append(remote(own.at[n, block, :, halves[h]], fromx.at[n, 1 - h, :, halves[h]],
                                  dir_send.at[n, h], dir_recv.at[n, h], target))
            directs[-1].start()
        for h, block in ((0, right), (1, left)):
            own[n, block, :, halves[h]] += got[n, block, :, halves[h]]
        own[n, x] += got[n, x]
    for n in range(2):
        for h, target, block in ((0, to_right, right), (1, to_left, left)):
            relays[2 * n + h].wait()
            own[n, block, :, halves[h]] += rel[n, h]
            combs.append(remote(own.at[n, block, :, halves[h]], fromx.at[n, h, :, halves[h]],
                                comb_send.at[n, h], comb_recv.at[n, h], target))
            combs[-1].start()
    for n in range(2):
        for copy in directs[2 * n:2 * n + 2] + combs[2 * n:2 * n + 2]:
            copy.wait()
        for jhi in range(14):
            lanes = slice(jhi * 128, (jhi + 1) * 128)
            ybuf[n, pl.ds(jhi, 16, stride=16), :] = own[n, x, :, lanes] + (fromx[n, 0, :, lanes] + fromx[n, 1, :, lanes])
        for d in range(1, 16):
            peer = (ch + d) % 16
            outs.append(remote(ybuf.at[n, pl.ds(pl.multiple_of(peer * 16, 16), 16)], z_ref.at[n, here],
                               out_send.at[n, d], out_recv.at[n, d], {"ch": peer}))
            outs[-1].start()
        z_ref[n, here] = ybuf[n, here]
    for copy in list_copies + outs:
        copy.wait()


def exchange(surf, he, own_list):
    dma = pltpu.SemaphoreType.DMA
    return pl.pallas_call(
        exchange_kernel,
        out_shape=(jax.ShapeDtypeStruct((2, 256, 128), f32), jax.ShapeDtypeStruct((256, 128), i32)),
        in_specs=[ANY, VM, VM],
        out_specs=(VM, VM),
        scratch_shapes=[pltpu.VMEM((1792, 128), f32), pltpu.VMEM((2, 4, 16, 1792), f32), pltpu.VMEM((2, 4, 16, 1792), f32),
                        pltpu.VMEM((2, 4, 16, 1792), f32), pltpu.VMEM((2, 2, 16, HALF), f32),
                        pltpu.VMEM((2, 2, 16, 1792), f32), pltpu.VMEM((2, 256, 128), f32),
                        dma, dma((2,)), dma((2,)), dma((2, 2)), dma((2, 2)), dma((2, 2)), dma((2, 2)),
                        dma((2, 2)), dma((2, 2)), dma((2, 16)), dma((2, 16)), dma((16,)), dma((16,))],
        compiler_params=pltpu.CompilerParams(vmem_limit_bytes=40 * 2**20, collective_id=0, has_side_effects=True),
        name="exchange",
    )(surf, he, own_list)


def spread_kernel(rows, es_ref, z_ref, l_ref, lev_ref, bv_ref, bs_ref, mp_ref, prev_hbm, coup_ref,
                  amp_hbm, spec_ref,
                  prev, ampo, ahi, alo, psem, asem):
    step = pl.program_id(0)
    steps = pl.num_programs(0)
    chunk = 128
    nchunk = NCH // chunk

    def prev_copy(i):
        return pltpu.make_async_copy(prev_hbm.at[pl.ds(i * chunk, chunk)], prev.at[pl.ds(i * chunk, chunk)], psem.at[i])

    def amp_copy(i):
        return pltpu.make_async_copy(ampo.at[pl.ds(i * chunk, chunk)], amp_hbm.at[pl.ds(i * chunk, chunk)], asem.at[i])

    @pl.when(step == 0)
    def _():
        for i in range(nchunk):
            prev_copy(i).start()
        z = [z_ref[0], z_ref[1]]
        pieces = []
        for a in z:
            hi, lo = split2(a)
            pieces.append((hi, lo))
        order = [pieces[0][0], pieces[1][0], pieces[0][1], pieces[1][1]]
        rights = []
        for jlo in range(4):
            parts = [a[:, jlo * 32:(jlo + 1) * 32] for a in order]
            one = jnp.concatenate(parts, axis=1)
            rights.append(jnp.concatenate([one, one], axis=1).astype(bf16))
        lt = jnp.transpose(l_ref[...])
        lev = lev_ref[...]
        io = lax.broadcasted_iota(i32, (128, NCH), 0)
        sel = ((io % 32 == jnp.broadcast_to(lev, (128, NCH))) & (io < 96)).astype(f32)
        selt = jnp.transpose(sel).astype(bf16)
        def three(t):
            a, r = split2(t)
            b, r = split2(r)
            return jnp.concatenate([a, b, r, jnp.zeros_like(a)], axis=0).astype(bf16)
        table = jnp.concatenate([three(bv_ref[...]), three(bs_ref[...])], axis=1)
        momenta = (lax.broadcasted_iota(i32, (8, 256), 1).astype(f32) + 0.5) * (momentum_top / 256)
        times = lax.broadcasted_iota(i32, (8, 256), 0).astype(f32) * time_step
        zeros = jnp.zeros((8, 128), f32)
        facts = []
        for n in range(2):
            ang = es_ref[0, n] * times + 0.5 * times * (momenta * momenta) + (es_ref[1, n] + mp_ref[...])
            co = (0.5 * time_step) * jnp.cos(ang)
            si = (0.5 * time_step) * jnp.sin(ang)
            for khi in range(2):
                c, s = co[:, khi * 128:(khi + 1) * 128], si[:, khi * 128:(khi + 1) * 128]
                blk = jnp.concatenate([jnp.concatenate([c, s], 1), jnp.concatenate([-s, c], 1)], 0)
                hi, lo = split2(blk)
                z16 = jnp.zeros((16, 256), f32)
                for d in range(2):
                    def piece(b):
                        own = [z16, z16]
                        own[d] = b
                        two = [z16, z16] * 2
                        two[2 * n], two[2 * n + 1] = own
                        return two
                    rowsl = piece(hi) + piece(hi) + piece(lo) + piece(lo)
                    facts.append(jnp.concatenate(rowsl, axis=0).astype(bf16))
        for i in range(nchunk):
            rs = pl.ds(i * chunk, chunk)
            ioc = lax.broadcasted_iota(i32, (chunk, 256), 0) + i * chunk
            r = None
            for jlo in range(4):
                one = (ioc == jnp.broadcast_to(lt[jlo * 32:jlo * 32 + 1, :], (chunk, 256))).astype(f32).astype(bf16)
                t = dot(one, rights[jlo])
                r = t if r is None else r + t
            left = r.astype(bf16)
            bt = dot(selt[i * chunk:(i + 1) * chunk], table)
            prev_copy(i).wait()
            for n in range(2):
                for khi in range(2):
                    su = dot(left, facts[(n * 2 + khi) * 2])
                    de = dot(left, facts[(n * 2 + khi) * 2 + 1])
                    bvc = bt[:, khi * 128:(khi + 1) * 128]
                    bsc = bt[:, 256 + khi * 128:256 + (khi + 1) * 128]
                    for p in range(2):
                        sidx = n * 4 + khi * 2 + p
                        fr = bvc * de[:, p * 128:(p + 1) * 128] - bsc * su[:, p * 128:(p + 1) * 128]
                        am = prev[rs, sidx, :] + fr
                        ampo[rs, sidx, :] = am
                        h = am.astype(bf16)
                        ahi[rs, sidx * 128:(sidx + 1) * 128] = h
                        alo[rs, sidx * 128:(sidx + 1) * 128] = (am - h.astype(f32)).astype(bf16)
            amp_copy(i).start()

    c = coup_ref[...]
    chi = c.astype(bf16)
    clo = (c - chi.astype(f32)).astype(bf16)
    for s in range(4):
        cs = slice(s * 256, (s + 1) * 256)
        both = dot(jnp.concatenate([chi, clo], 0), ahi[:, cs])
        res = both[:rows] + both[rows:] + dot(chi, alo[:, cs])
        spec_ref[:, 2 * s, :] = res[:, :128]
        spec_ref[:, 2 * s + 1, :] = res[:, 128:]

    @pl.when(step == steps - 1)
    def _():
        for i in range(nchunk):
            amp_copy(i).wait()

def spread(es, z, lists, lev, bv, bs, mp, prev, coup, rows=256):
    return pl.pallas_call(
        functools.partial(spread_kernel, rows),
        grid=(NG // rows,),
        out_shape=(jax.ShapeDtypeStruct((NCH, 8, 128), f32), jax.ShapeDtypeStruct((NG, 8, 128), f32)),
        in_specs=[SM, VM, VM, VM, VM, VM, VM, ANY, pl.BlockSpec((rows, NCH), lambda i: (i, 0))],
        out_specs=(ANY, pl.BlockSpec((rows, 8, 128), lambda i: (i, 0, 0))),
        scratch_shapes=[pltpu.VMEM((NCH, 8, 128), f32), pltpu.VMEM((NCH, 8, 128), f32),
                        pltpu.VMEM((NCH, 1024), bf16), pltpu.VMEM((NCH, 1024), bf16),
                        pltpu.SemaphoreType.DMA((7,)), pltpu.SemaphoreType.DMA((7,))],
        compiler_params=pltpu.CompilerParams(vmem_limit_bytes=56 * 2**20),
        cost_estimate=pl.CostEstimate(flops=3*2*2048*896*1024, bytes_accessed=24*2**20, transcendentals=0),
        name="spread",
    )(es, z, lists, lev, bv, bs, mp, prev, coup)


def shards(surface_rows, he_states, energies, state_phase, momentum_phase, bessel_value, bessel_slope,
           channel_l2, surface_list, previous, coupling):
    surf = surface_rows.reshape(1792, 128)
    he = he_states.reshape(4, 2, 32, 128)
    own_list = jnp.repeat(jnp.pad(surface_list.reshape(14, 4), ((0, 2), (0, 0)), constant_values=-1), 32, axis=1)
    projected, listed = exchange(surf, he, own_list)
    first = (lax.axis_index("row") * 16 + lax.axis_index("ch")) * 2
    states = jnp.stack([lax.dynamic_slice_in_dim(energies, first, 2, 0), lax.dynamic_slice_in_dim(state_phase, first, 2, 0)])
    prev = previous.reshape(NCH, 2, 2, 2, 128).transpose(0, 1, 3, 2, 4).reshape(NCH, 8, 128)
    amplitudes, spectrum = spread(states, projected, listed, channel_l2.reshape(1, NCH), bessel_value, bessel_slope,
                                  momentum_phase.reshape(1, 256), prev, coupling)

    def whole(a):
        return a.reshape(-1, 2, 2, 2, 128).transpose(0, 1, 3, 2, 4).reshape(-1, 2, 2, 256)

    return whole(amplitudes), whole(spectrum)


def solution(mesh):
    split = P(None, ("row", "ch"), None, None)
    return jax.shard_map(
        shards,
        mesh=mesh,
        in_specs=(P(None, None, "ch", "row"), P(None, "row"), P(), P(), P(), P(), P(), P(), P("ch"), split, P()),
        out_specs=(split, split),
        check_vma=False,
    )
```

profile of v0, /device:TPU:0, one launch (start us, length us, event | category | flops | bytes accessed | tf_op | source)
XLA Modules:
  0.0 61.5 jit_solution(2194221920475592484)
XLA Ops:
  0.6 0.8 %dynamic-slice_bitcast_fusion = (f32[1,2]{1,0:T(1,128)S(1)}, f32[1,2]{1,0:T(1,128)S(1)}) fusion(f32[256]{0:T(256)} %param.14, s32[]{:T(128)S(6)} %select_n.4, f32[256]{0:T(256)} %param.13), kind=kLoop, calls=%fused_computation.1 | loop fusion | bytes 36 | tf_op jit(solution)/shard_map/stack | solution.py:268
  1.4 0.6 pad_maximum_fusion.es_ref
  2.0 1.3 %reshape.44.lev_ref = s32[1,896]{1,0:T(1,128)} reshape(s32[896]{0:T(1024)} %param.18) | data formatting | bytes 7168 | tf_op jit(solution)/shard_map/reshape | solution.py:270
  3.3 0.7 %reshape.42 = s32[14,4]{1,0:T(8,128)S(1)} reshape(s32[56]{0:T(128)} %param.19) | data formatting | bytes 448 | tf_op jit(solution)/shard_map/reshape | solution.py:265
  4.0 0.1 broadcast_in_dim.3
  4.1 0.1 reshape.43.own_list
  4.2 0.0 copy-start
  4.2 1.2 %copy-done = f32[4,8,56,128]{3,2,1,0:T(8,128)S(1)} copy-done((f32[4,8,56,128]{3,2,1,0:T(8,128)S(1)}, f32[4,8,56,128]{3,2,1,0:T(8,128)}, u32[]{:S(2)}) %copy-start) | copy-done | bytes 917528
  5.4 0.0 copy-start.1
  5.4 0.9 %copy-done.1 = f32[256,128]{1,0:T(8,128)S(1)} copy-done((f32[256,128]{1,0:T(8,128)S(1)}, f32[256,128]{1,0:T(8,128)}, u32[]{:S(2)}) %copy-start.1) | copy-done | bytes 131096
  6.3 25.8 %exchange.1 = (f32[2,256,128]{2,1,0:T(8,128)S(1)}, s32[256,128]{1,0:T(8,128)S(1)}) custom-call(f32[1792,128]{1,0:T(8,128)S(1)} %bitcast.22, f32[4,2,32,128]{3,2,1,0:T(8,128)S(1)} %bitcast.23, s32[16,128]{1,0:T(8,128)S(1)} %reshape.43.own_list), custom_call_target="tpu_custom_call" | custom-call | tf_op jit(solution)/shard_map/exchange/pallas_call | solution.py:127
  32.1 0.0 copy-start.2
  32.1 0.7 %copy-done.2 = f32[2,256,128]{2,1,0:T(8,128)} copy-done((f32[2,256,128]{2,1,0:T(8,128)}, f32[2,256,128]{2,1,0:T(8,128)S(1)}, u32[]{:S(2)}) %copy-start.2) | copy-done | bytes 262168
  32.8 0.0 copy-start.3
  32.8 0.6 %copy-done.3 = s32[256,128]{1,0:T(8,128)} copy-done((s32[256,128]{1,0:T(8,128)}, s32[256,128]{1,0:T(8,128)S(1)}, u32[]{:S(2)}) %copy-start.3) | copy-done | bytes 131096
  33.4 28.0 %spread.1 = (f32[896,8,128]{2,1,0:T(8,128)}, f32[2048,8,128]{2,1,0:T(8,128)}) custom-call(f32[2,2]{1,0:T(2,128)} %pad_maximum_fusion.es_ref, f32[2,256,128]{2,1,0:T(8,128)} %copy-done.2, s32[256,128]{1,0:T(8,128)} %copy-done.3, s32[1,896]{1,0:T(1,128)} %reshape.44.lev_ref, f32[32,256]{1,0:T(8,128)} %bv_ref.1, f32[32,256]{1,0:T(8,128)} %bs_ref.1, ...), custom_call_target="tpu_custom_call" | custom-call | flops 11274289152 | bytes 25165824 | tf_op jit(solution)/shard_map/spread/pallas_call | solution.py:246
  (1 shorter events, 0.0 us)
Async XLA Ops:
  4.2 1.2 %copy-start = (f32[4,8,56,128]{3,2,1,0:T(8,128)S(1)}, f32[4,8,56,128]{3,2,1,0:T(8,128)}, u32[]{:S(2)}) copy-start(f32[4,8,56,128]{3,2,1,0:T(8,128)} %param.11) | copy-start | bytes 2752516
  5.4 0.9 %copy-start.1 = (f32[256,128]{1,0:T(8,128)S(1)}, f32[256,128]{1,0:T(8,128)}, u32[]{:S(2)}) copy-start(f32[256,128]{1,0:T(8,128)} %param.12) | copy-start | bytes 393220
  32.1 0.7 %copy-start.2 = (f32[2,256,128]{2,1,0:T(8,128)}, f32[2,256,128]{2,1,0:T(8,128)S(1)}, u32[]{:S(2)}) copy-start(f32[2,256,128]{2,1,0:T(8,128)S(1)} %get-tuple-element.6.z_ref) | copy-start | bytes 786436
  32.8 0.6 %copy-start.3 = (s32[256,128]{1,0:T(8,128)}, s32[256,128]{1,0:T(8,128)S(1)}, u32[]{:S(2)}) copy-start(s32[256,128]{1,0:T(8,128)S(1)} %get-tuple-element.7.l_ref) | copy-start | bytes 393220
where the time goes:
time: 61.8 us; the launch traced here: 61.5 us
  Pallas kernels  53.8 us (87%)
  local copies, waits for them, and re-layouts  6.38 us (10%)
  between operations  0.67 us (1%)
    pallas_call x1, Pallas kernels, spread(): pl.pallas_call(functools.partial(spread_kernel, rows), grid=(NG // rows,)...  28 us
    pallas_call x1, Pallas kernels, exchange(): pl.pallas_call(exchange_kernel, out_shape=(jax.ShapeDtypeStruct((2, 256,...  25.8 us
    unnamed x8, local copies, waits for them, and re-layouts  3.43 us
    reshape x1, local copies, waits for them, and re-layouts, shards(): channel_l2.reshape(1, NCH)  1.27 us

commit v1 on v0

v1 whole, which is shorter than its diff:
```python
import jax
import jax.numpy as jnp
from jax import lax
from jax.experimental import pallas as pl
from jax.experimental.pallas import tpu as pltpu
from jax.sharding import PartitionSpec as P

f32, bf16, i32 = jnp.float32, jnp.bfloat16, jnp.int32
time_step, momentum_top = 0.4, 2.0
NCH, NG = 896, 2048
HALF = 896
PART = 256
ANY = pl.BlockSpec(memory_space=pl.ANY)
VM = pl.BlockSpec(memory_space=pltpu.VMEM)
HBM = pl.BlockSpec(memory_space=pltpu.HBM)
MESH = pl.DeviceIdType.MESH
NT = (((1,), (1,)), ((), ()))


def split2(x):
    hi = x.astype(bf16).astype(f32)
    return hi, x - hi


def dot(a, b):
    return lax.dot_general(a, b, (((1,), (0,)), ((), ())), preferred_element_type=f32)


def exchange_kernel(surf_hbm, he_hbm, list_hbm, energy_hbm, phase_hbm, mp_hbm, bv_hbm, bs_hbm, lev_hbm, prev_hbm,
                    coup_hbm, z_ref, hot_ref, bt_ref, fact_ref, left_ref, prev_ref,
                    own_s, he_v, list_ref, energy_ref, phase_ref, mp_v, bv_v, bs_v, lev_v, stage, other, own, got, rel, fromx, ybuf, own_list, lists,
                    load_sem, prev_sem, coup_sem, core_send, core_recv, rel_send, rel_recv,
                    dir_send, dir_recv, comb_send, comb_recv, out_send, out_recv, list_send, list_recv):
    row, ch = lax.axis_index("row"), lax.axis_index("ch")
    x, core = row // 2, row % 2
    right, left, across = (x + 1) % 4, (x + 3) % 4, (x + 2) % 4
    partner = {"row": 2 * x + 1 - core}
    to_right, to_left = {"row": 2 * right + core}, {"row": 2 * left + core}

    loads = [pltpu.make_async_copy(src, dst, load_sem.at[k]) for k, (src, dst) in enumerate((
        (he_hbm, he_v), (surf_hbm, own_s), (list_hbm, list_ref), (energy_hbm, energy_ref), (phase_hbm, phase_ref),
        (mp_hbm, mp_v), (bv_hbm, bv_v), (bs_hbm, bs_v), (lev_hbm, lev_v)))]
    for load in loads:
        load.start()
    barrier = pltpu.get_barrier_semaphore()
    for target in (partner, to_right, to_left):
        pl.semaphore_signal(barrier, inc=1, device_id=target, device_id_type=MESH)
    for d in range(1, 16):
        pl.semaphore_signal(barrier, inc=1, device_id={"ch": (ch + d) % 16}, device_id_type=MESH)

    def coup_copy(k):
        return pltpu.make_async_copy(coup_hbm.at[pl.ds(k * PART, PART)], stage.at[k % 2], coup_sem.at[k % 2])

    prev_copies = [pltpu.make_async_copy(prev_hbm.at[:, s, :], prev_ref.at[:, pl.ds(s * 128, 128)], prev_sem.at[s])
                   for s in range(8)]

    loads[0].wait()
    parts = []
    for side in (1 - core, core):
        for n in range(2):
            for xx in range(4):
                parts.append(he_v[xx, side, pl.ds(n, 16, stride=2), :])
    he = jnp.concatenate(parts, axis=0)
    h_hi, h_lo = split2(he)
    h_left = jnp.concatenate([h_hi, h_hi, h_lo], axis=1).astype(bf16)
    loads[1].wait()
    for k in range(2):
        coup_copy(k).start()
    for copy in prev_copies:
        copy.start()
    for jc in range(7):
        rows = jnp.concatenate([own_s[pl.ds(jc * 8 + j, 32, stride=56), :] for j in range(8)], axis=0)
        s_hi, s_lo = split2(rows)
        s_right = jnp.concatenate([s_hi, s_lo, s_hi], axis=1).astype(bf16)
        part = lax.dot_general(h_left, s_right, NT, preferred_element_type=f32)
        lanes = slice(jc * 256, (jc + 1) * 256)
        for n in range(2):
            for xx in range(4):
                at = (n * 4 + xx) * 16
                other[n, xx, :, lanes] = part[at:at + 16]
                own[n, xx, :, lanes] = part[128 + at:144 + at]

    place = lax.broadcasted_iota(i32, (16, 128), 0) * 4 + lax.broadcasted_iota(i32, (16, 128), 1) // 32
    listed = jnp.full((16, 128), -1, i32)
    loads[2].wait()
    for j in range(56):
        listed = jnp.where(place == j, list_ref[j], listed)
    own_list[...] = listed
    pl.semaphore_wait(barrier, 18)

    def remote(src, dst, send, recv, target):
        return pltpu.make_async_remote_copy(src_ref=src, dst_ref=dst, send_sem=send, recv_sem=recv,
                                            device_id=target, device_id_type=MESH)

    def core_copy(n, k):
        block = (across, right, left, x)[k]
        return remote(other.at[n, block], got.at[n, block], core_send.at[n, k], core_recv.at[n, k], partner)

    for n, k in ((0, 0), (0, 1), (0, 2), (1, 0), (1, 1), (1, 2), (0, 3), (1, 3)):
        core_copy(n, k).start()
    here = pl.ds(pl.multiple_of(ch * 16, 16), 16)
    list_copies = [remote(own_list, lists.at[here], list_send.at[d], list_recv.at[d], {"ch": (ch + d) % 16})
                   for d in range(1, 16)]

    halves = (pl.ds(0, HALF), pl.ds(HALF, HALF))
    relays, directs, combs, outs = [], [], [], []

    def add_core(n, k):
        block = (across, right, left, x)[k]
        core_copy(n, k).wait()
        own[n, block] += got[n, block]

    for n in range(2):
        add_core(n, 0)
        for h, target in ((0, to_right), (1, to_left)):
            relays.append(remote(own.at[n, across, :, halves[h]], rel.at[n, h], rel_send.at[n, h],
                                 rel_recv.at[n, h], target))
            relays[-1].start()
        for k, h, target, block in ((1, 1, to_right, right), (2, 0, to_left, left)):
            add_core(n, k)
            directs.append(remote(own.at[n, block, :, halves[h]], fromx.at[n, 1 - h, :, halves[h]],
                                  dir_send.at[n, h], dir_recv.at[n, h], target))
            directs[-1].start()
    for copy in list_copies:
        copy.start()
    lists[here] = listed
    for n in range(2):
        add_core(n, 3)

    for load in loads[3:]:
        load.wait()
    momenta = (lax.broadcasted_iota(i32, (8, 256), 1).astype(f32) + 0.5) * (momentum_top / 256)
    times = lax.broadcasted_iota(i32, (8, 256), 0).astype(f32) * time_step
    z16 = jnp.zeros((16, 256), f32)
    first = (row * 16 + ch) * 2
    for n in range(2):
        angle = energy_ref[first + n] * times + 0.5 * times * (momenta * momenta) + (phase_ref[first + n] + mp_v[...])
        cos, sin = (0.5 * time_step) * jnp.cos(angle), (0.5 * time_step) * jnp.sin(angle)
        for khi in range(2):
            c, s = cos[:, khi * 128:(khi + 1) * 128], sin[:, khi * 128:(khi + 1) * 128]
            block = jnp.concatenate([jnp.concatenate([c, s], 1), jnp.concatenate([-s, c], 1)], 0)
            for d in range(2):
                spread_rows = []
                for piece in split2(block):
                    four = [z16] * 4
                    four[2 * n + d] = piece
                    spread_rows += four * 2
                fact_ref[(n * 2 + khi) * 2 + d] = jnp.concatenate(spread_rows, axis=0).astype(bf16)

    def three(table):
        a, rest = split2(table)
        b, rest = split2(rest)
        return jnp.concatenate([a, b, rest, jnp.zeros_like(a)], axis=0).astype(bf16)

    table = jnp.concatenate([three(bv_v[...]), three(bs_v[...])], axis=1)
    level_of = lax.broadcasted_iota(i32, (128, 128), 0)
    for i in range(7):
        chosen = (level_of % 32 == jnp.broadcast_to(lev_v[i:i + 1, :], (128, 128))) & (level_of < 96)
        bt_ref[i * 128:(i + 1) * 128, :] = dot(jnp.transpose(chosen.astype(f32)).astype(bf16), table)

    def split_coupling(k):
        coup_copy(k).wait()

        def some(i, _):
            at = pl.multiple_of(i * 32, 32)
            c = stage[k % 2, pl.ds(at, 32), :]
            hi = c.astype(bf16)
            to = pl.ds(pl.multiple_of(k * PART + i * 32, 32), 32)
            left_ref[to, 0:NCH] = hi
            left_ref[to, NCH:2 * NCH] = (c - hi.astype(f32)).astype(bf16)
            left_ref[to, 2 * NCH:3 * NCH] = hi
            return 0

        lax.fori_loop(0, PART // 32, some, 0)
        if k + 2 < NG // PART:
            coup_copy(k + 2).start()

    split_coupling(0)
    split_coupling(1)
    for n in range(2):
        for h, target, block in ((0, to_right, right), (1, to_left, left)):
            relays[2 * n + h].wait()
            own[n, block, :, halves[h]] += rel[n, h]
            combs.append(remote(own.at[n, block, :, halves[h]], fromx.at[n, h, :, halves[h]],
                                comb_send.at[n, h], comb_recv.at[n, h], target))
            combs[-1].start()
        split_coupling(2 + n)

    for copy in list_copies:
        copy.wait()
    row_of = jnp.transpose(lists[...])
    for i in range(7):
        channel = lax.broadcasted_iota(i32, (128, 256), 0) + i * 128
        for jlo in range(4):
            match = channel == jnp.broadcast_to(row_of[jlo * 32:jlo * 32 + 1, :], (128, 256))
            hot_ref[i * 128:(i + 1) * 128, jlo * 256:(jlo + 1) * 256] = match.astype(f32).astype(bf16)
    for n in range(2):
        for tail in (14, 15):
            ybuf[n, pl.ds(tail, 16, stride=16), :] = jnp.zeros((16, 128), f32)
    for n in range(2):
        for copy in directs[2 * n:2 * n + 2] + combs[2 * n:2 * n + 2]:
            copy.wait()
        for jhi in range(14):
            lanes = slice(jhi * 128, (jhi + 1) * 128)
            ybuf[n, pl.ds(jhi, 16, stride=16), :] = own[n, x, :, lanes] + (fromx[n, 0, :, lanes] + fromx[n, 1, :, lanes])
        for d in range(1, 16):
            peer = (ch + d) % 16
            outs.append(remote(ybuf.at[n, pl.ds(pl.multiple_of(peer * 16, 16), 16)], z_ref.at[n, here],
                               out_send.at[n, d], out_recv.at[n, d], {"ch": peer}))
            outs[-1].start()
        z_ref[n, here] = ybuf[n, here]
        split_coupling(4 + 2 * n)
        split_coupling(5 + 2 * n)
    for copy in prev_copies:
        copy.wait()
    for copy in outs:
        copy.wait()


def exchange(*operands):
    dma = pltpu.SemaphoreType.DMA
    block = pltpu.VMEM((2, 4, 16, 1792), f32)
    return pl.pallas_call(
        exchange_kernel,
        out_shape=(jax.ShapeDtypeStruct((2, 256, 128), f32), jax.ShapeDtypeStruct((NCH, 1024), bf16),
                   jax.ShapeDtypeStruct((NCH, 512), f32), jax.ShapeDtypeStruct((8, 256, 256), bf16),
                   jax.ShapeDtypeStruct((NG, 3 * NCH), bf16), jax.ShapeDtypeStruct((NCH, 1024), f32)),
        in_specs=[HBM] * 11,
        out_specs=(VM,) * 6,
        scratch_shapes=[pltpu.VMEM((1792, 128), f32), pltpu.VMEM((4, 2, 32, 128), f32), pltpu.SMEM((56,), i32),
                        pltpu.SMEM((256,), f32), pltpu.SMEM((256,), f32), pltpu.VMEM((1, 256), f32),
                        pltpu.VMEM((32, 256), f32), pltpu.VMEM((32, 256), f32), pltpu.VMEM((7, 128), i32),
                        pltpu.VMEM((2, PART, NCH), f32), block, block, block,
                        pltpu.VMEM((2, 2, 16, HALF), f32), pltpu.VMEM((2, 2, 16, 1792), f32), pltpu.VMEM((2, 256, 128), f32),
                        pltpu.VMEM((16, 128), i32), pltpu.VMEM((256, 128), i32),
                        dma((9,)), dma((8,)), dma((2,)), dma((2, 4)), dma((2, 4)), dma((2, 2)), dma((2, 2)),
                        dma((2, 2)), dma((2, 2)), dma((2, 2)), dma((2, 2)), dma((2, 16)), dma((2, 16)), dma((16,)), dma((16,))],
        compiler_params=pltpu.CompilerParams(vmem_limit_bytes=20 * 2**20, collective_id=0, has_side_effects=True),
        cost_estimate=pl.CostEstimate(flops=10**8, bytes_accessed=14 * 2**20, transcendentals=0),
        name="exchange",
    )(*(pltpu.with_memory_space_constraint(a, pltpu.HBM) for a in operands))


def spread_kernel(z_ref, hot_ref, bt_ref, fact_ref, left_ref, prev_ref, amp_hbm, spec_hbm,
                  right, ampo, obuf, asem, osem):
    chunk, mrows, slots = 128, 512, 4
    nchunk = NCH // chunk
    (hi0, lo0), (hi1, lo1) = split2(z_ref[0]), split2(z_ref[1])
    picks = []
    for jlo in range(4):
        one = jnp.concatenate([a[:, jlo * 32:(jlo + 1) * 32] for a in (hi0, hi1, lo0, lo1)], axis=1)
        picks.append(jnp.concatenate([one, one], axis=1).astype(bf16))
    picks = jnp.concatenate(picks, axis=0)

    def amp_copy(s):
        return pltpu.make_async_copy(ampo.at[:, pl.ds(s * 128, 128)], amp_hbm.at[:, s, :], asem.at[s])

    for i in range(nchunk):
        at = pl.ds(i * chunk, chunk)
        chosen = dot(hot_ref[at, :], picks).astype(bf16)
        for n in range(2):
            for khi in range(2):
                surf = dot(chosen, fact_ref[(n * 2 + khi) * 2])
                slope = dot(chosen, fact_ref[(n * 2 + khi) * 2 + 1])
                value_at = bt_ref[at, khi * 128:(khi + 1) * 128]
                slope_at = bt_ref[at, 256 + khi * 128:256 + (khi + 1) * 128]
                for p in range(2):
                    s = n * 4 + khi * 2 + p
                    lanes = slice(p * 128, (p + 1) * 128)
                    cols = slice(s * 128, (s + 1) * 128)
                    total = prev_ref[at, cols] + (value_at * slope[:, lanes] - slope_at * surf[:, lanes])
                    ampo[at, cols] = total
                    hi = total.astype(bf16)
                    right[at, cols] = hi
                    right[pl.ds(NCH + i * chunk, chunk), cols] = hi
                    right[pl.ds(2 * NCH + i * chunk, chunk), cols] = (total - hi.astype(f32)).astype(bf16)
    for s in range(8):
        amp_copy(s).start()

    def out_copy(u, s):
        n, m = todo[u]
        return pltpu.make_async_copy(obuf.at[u % slots, :, pl.ds(s * 128, 128)],
                                     spec_hbm.at[pl.ds(m * mrows, mrows), 4 * n + s, :], osem.at[u % slots, s])

    todo = [(n, m) for n in range(2) for m in range(NG // mrows)]
    for u, (n, m) in enumerate(todo):
        if u >= slots:
            for s in range(4):
                out_copy(u - slots, s).wait()
        obuf[u % slots] = dot(left_ref[m * mrows:(m + 1) * mrows, :], right[:, n * 512:(n + 1) * 512])
        for s in range(4):
            out_copy(u, s).start()
    for u in range(len(todo) - slots, len(todo)):
        for s in range(4):
            out_copy(u, s).wait()
    for s in range(8):
        amp_copy(s).wait()


def spread(*operands):
    dma = pltpu.SemaphoreType.DMA
    return pl.pallas_call(
        spread_kernel,
        out_shape=(jax.ShapeDtypeStruct((NCH, 8, 128), f32), jax.ShapeDtypeStruct((NG, 8, 128), f32)),
        in_specs=[VM] * 6,
        out_specs=(ANY, ANY),
        scratch_shapes=[pltpu.VMEM((3 * NCH, 1024), bf16), pltpu.VMEM((NCH, 1024), f32), pltpu.VMEM((4, 512, 512), f32),
                        dma((8,)), dma((4, 4))],
        compiler_params=pltpu.CompilerParams(vmem_limit_bytes=20 * 2**20),
        cost_estimate=pl.CostEstimate(flops=3 * 2 * NG * NCH * 1024, bytes_accessed=12 * 2**20, transcendentals=0),
        name="spread",
    )(*operands)


def shards(surface_rows, he_states, energies, state_phase, momentum_phase, bessel_value, bessel_slope,
           channel_l2, surface_list, previous, coupling):
    prev = previous.reshape(NCH, 2, 2, 2, 128).transpose(0, 1, 3, 2, 4).reshape(NCH, 8, 128)
    ready = exchange(surface_rows.reshape(1792, 128), he_states.reshape(4, 2, 32, 128), surface_list, energies, state_phase,
                     momentum_phase.reshape(1, 256), bessel_value, bessel_slope, channel_l2.reshape(7, 128), prev, coupling)
    amplitudes, spectrum = spread(*ready)

    def whole(a):
        return a.reshape(-1, 2, 2, 2, 128).transpose(0, 1, 3, 2, 4).reshape(-1, 2, 2, 256)

    return whole(amplitudes), whole(spectrum)


def solution(mesh):
    split = P(None, ("row", "ch"), None, None)
    return jax.shard_map(
        shards,
        mesh=mesh,
        in_specs=(P(None, None, "ch", "row"), P(None, "row"), P(), P(), P(), P(), P(), P(), P("ch"), split, P()),
        out_specs=(split, split),
        check_vma=False,
    )
```

time: 61.8 us -> 43.8 us (0.71)
  Pallas kernels: 53.8 us -> 42.9 us
  local copies, waits for them, and re-layouts: 6.38 us -> 0 us
    pallas_call x1, Pallas kernels: 28 us -> 17.5 us  [spread(): pl.pallas_call(spread_kernel, out_shape=(jax.ShapeDtypeStruct((NCH, 8, 12...]
    unnamed x8 -> x0, local copies, waits for them, and re-layouts: 3.43 us -> none
    reshape x3 -> x0, local copies, waits for them, and re-layouts: 2.09 us -> none  [the longest x1 1.27 us: shards(): channel_l2.reshape(1, NCH)]
    another operation x1 -> x0, local copies, waits for them, and re-layouts: 0.77 us -> none  [shards(): jnp.stack([lax.dynamic_slice_in_dim(energies, first, 2, 0), lax.dynamic_s...]
where the time goes in v1:
time: 43.8 us; the launch traced here: 43.5 us
  Pallas kernels  42.9 us (98%)
  between operations  0.64 us (1%)
    pallas_call x1, Pallas kernels, exchange(): pl.pallas_call(exchange_kernel, out_shape=(jax.ShapeDtypeStruct((2, 256,...  25.4 us
    pallas_call x1, Pallas kernels, spread(): pl.pallas_call(spread_kernel, out_shape=(jax.ShapeDtypeStruct((NCH, 8, 12...  17.5 us

profile of v1, /device:TPU:0, one launch (start us, length us, event | category | flops | bytes accessed | tf_op | source)
XLA Modules:
  0.0 43.5 jit_solution(267015396349794564)
XLA Ops:
  0.6 25.4 %exchange.1 = (f32[2,256,128]{2,1,0:T(8,128)S(1)}, bf16[896,1024]{1,0:T(8,128)(2,1)S(1)}, f32[896,512]{1,0:T(8,128)S(1)}, bf16[8,256,256]{2,1,0:T(8,128)(2,1)S(1...) custom-call(f32[1792,128]{1,0:T(8,128)} %bitcast.20, f32[4,2,32,128]{3,2,1,0:T(8,128)} %bitcast.21, ...), custom_call_target="tpu_custom_call" | custom-call | flops 100000000 | bytes 14680064 | tf_op jit(solution)/shard_map/exchange/pallas_call | solution.py:223
  26.1 17.5 %spread.1 = (f32[896,8,128]{2,1,0:T(8,128)}, f32[2048,8,128]{2,1,0:T(8,128)}) custom-call(f32[2,256,128]{2,1,0:T(8,128)S(1)} %get-tuple-element.10.z_ref, bf16[896,1024]{1,0:T(8,128)(2,1)S(1)} %get-tuple-element.11.hot_ref, f32[896,512]{1,0:T(8,128)S(1)} %get-tuple-element.12.bt_ref, bf16[8,256,256]{2,1,0:T(8,128)(2,1)S(1)} %get-tuple-element.13.fact_ref, ...), custom_call_target="tpu_custom_call" | custom-call | flops 11274289152 | bytes 12582912 | tf_op jit(solution)/shard_map/spread/pallas_call | solution.py:302

commit v2 on v1

v2 whole, which is shorter than its diff:
```python
import jax
import jax.numpy as jnp
from jax import lax
from jax.experimental import pallas as pl
from jax.experimental.pallas import tpu as pltpu
from jax.sharding import PartitionSpec as P

f32, bf16, i32 = jnp.float32, jnp.bfloat16, jnp.int32
time_step, momentum_top = 0.4, 2.0
NCH, NG = 896, 2048
HALF = 896
PART = 256
ANY = pl.BlockSpec(memory_space=pl.ANY)
VM = pl.BlockSpec(memory_space=pltpu.VMEM)
HBM = pl.BlockSpec(memory_space=pltpu.HBM)
MESH = pl.DeviceIdType.MESH
NT = (((1,), (1,)), ((), ()))


def split2(x):
    hi = x.astype(bf16).astype(f32)
    return hi, x - hi


def dot(a, b):
    return lax.dot_general(a, b, (((1,), (0,)), ((), ())), preferred_element_type=f32)


def exchange_kernel(surf_hbm, he_hbm, list_hbm, energy_hbm, phase_hbm, mp_hbm, bv_hbm, bs_hbm, lev_hbm, prev_hbm,
                    coup_hbm, left_ref, right_ref, first_ref, amp_ref,
                    own_s, he_v, list_ref, energy_ref, phase_ref, mp_v, bv_v, bs_v, lev_v, stage, other, own, got, rel, fromx, ybuf, own_list, lists, z_ref, hot_ref, bt_ref, fact_ref,
                    prev_ref, right_first, load_sem, prev_sem, coup_sem, core_send, core_recv, rel_send, rel_recv,
                    dir_send, dir_recv, comb_send, comb_recv, out_send, out_recv, list_send, list_recv):
    row, ch = lax.axis_index("row"), lax.axis_index("ch")
    x, core = row // 2, row % 2
    right, left, across = (x + 1) % 4, (x + 3) % 4, (x + 2) % 4
    partner = {"row": 2 * x + 1 - core}
    to_right, to_left = {"row": 2 * right + core}, {"row": 2 * left + core}

    loads = [pltpu.make_async_copy(src, dst, load_sem.at[k]) for k, (src, dst) in enumerate((
        (he_hbm, he_v), (surf_hbm, own_s), (list_hbm, list_ref), (energy_hbm, energy_ref), (phase_hbm, phase_ref),
        (mp_hbm, mp_v), (bv_hbm, bv_v), (bs_hbm, bs_v), (lev_hbm, lev_v)))]
    for load in loads:
        load.start()
    barrier = pltpu.get_barrier_semaphore()
    for target in (partner, to_right, to_left):
        pl.semaphore_signal(barrier, inc=1, device_id=target, device_id_type=MESH)
    for d in range(1, 16):
        pl.semaphore_signal(barrier, inc=1, device_id={"ch": (ch + d) % 16}, device_id_type=MESH)

    def coup_copy(k):
        return pltpu.make_async_copy(coup_hbm.at[pl.ds(k * PART, PART)], stage.at[k % 2], coup_sem.at[k % 2])

    prev_copies = [pltpu.make_async_copy(prev_hbm.at[:, s, :], prev_ref.at[:, pl.ds(s * 128, 128)], prev_sem.at[s])
                   for s in range(8)]

    loads[0].wait()
    parts = []
    for side in (1 - core, core):
        for n in range(2):
            for xx in range(4):
                parts.append(he_v[xx, side, pl.ds(n, 16, stride=2), :])
    he = jnp.concatenate(parts, axis=0)
    h_hi, h_lo = split2(he)
    h_left = jnp.concatenate([h_hi, h_hi, h_lo], axis=1).astype(bf16)
    loads[1].wait()
    for k in range(2):
        coup_copy(k).start()
    for copy in prev_copies:
        copy.start()
    for jc in range(7):
        rows = jnp.concatenate([own_s[pl.ds(jc * 8 + j, 32, stride=56), :] for j in range(8)], axis=0)
        s_hi, s_lo = split2(rows)
        s_right = jnp.concatenate([s_hi, s_lo, s_hi], axis=1).astype(bf16)
        part = lax.dot_general(h_left, s_right, NT, preferred_element_type=f32)
        lanes = slice(jc * 256, (jc + 1) * 256)
        for n in range(2):
            for xx in range(4):
                at = (n * 4 + xx) * 16
                other[n, xx, :, lanes] = part[at:at + 16]
                own[n, xx, :, lanes] = part[128 + at:144 + at]

    place = lax.broadcasted_iota(i32, (16, 128), 0) * 4 + lax.broadcasted_iota(i32, (16, 128), 1) // 32
    listed = jnp.full((16, 128), -1, i32)
    loads[2].wait()
    for j in range(56):
        listed = jnp.where(place == j, list_ref[j], listed)
    own_list[...] = listed
    pl.semaphore_wait(barrier, 18)

    def remote(src, dst, send, recv, target):
        return pltpu.make_async_remote_copy(src_ref=src, dst_ref=dst, send_sem=send, recv_sem=recv,
                                            device_id=target, device_id_type=MESH)

    def core_copy(n, k):
        block = (across, right, left, x)[k]
        return remote(other.at[n, block], got.at[n, block], core_send.at[n, k], core_recv.at[n, k], partner)

    for n, k in ((0, 0), (0, 1), (0, 2), (1, 0), (1, 1), (1, 2), (0, 3), (1, 3)):
        core_copy(n, k).start()
    here = pl.ds(pl.multiple_of(ch * 16, 16), 16)
    list_copies = [remote(own_list, lists.at[here], list_send.at[d], list_recv.at[d], {"ch": (ch + d) % 16})
                   for d in range(1, 16)]
    halves = (pl.ds(0, HALF), pl.ds(HALF, HALF))

    def add_core(n, k):
        block = (across, right, left, x)[k]
        core_copy(n, k).wait()
        own[n, block] += got[n, block]

    def relay(n, h):
        return remote(own.at[n, across, :, halves[h]], rel.at[n, h], rel_send.at[n, h], rel_recv.at[n, h],
                      (to_right, to_left)[h])

    def direct(n, h):
        block = (left, right)[h]
        return remote(own.at[n, block, :, halves[h]], fromx.at[n, 1 - h, :, halves[h]], dir_send.at[n, h],
                      dir_recv.at[n, h], (to_left, to_right)[h])

    def comb(n, h):
        block = (right, left)[h]
        return remote(own.at[n, block, :, halves[h]], fromx.at[n, h, :, halves[h]], comb_send.at[n, h],
                      comb_recv.at[n, h], (to_right, to_left)[h])

    def out(n, d):
        peer = (ch + d) % 16
        return remote(ybuf.at[n, pl.ds(pl.multiple_of(peer * 16, 16), 16)], z_ref.at[n, here],
                      out_send.at[n, d], out_recv.at[n, d], {"ch": peer})

    def ring_begin(n):
        add_core(n, 0)
        for h in range(2):
            relay(n, h).start()
        for k, h in ((1, 1), (2, 0)):
            add_core(n, k)
            direct(n, h).start()

    def ring_pass(n):
        for h, block in ((0, right), (1, left)):
            relay(n, h).wait()
            own[n, block, :, halves[h]] += rel[n, h]
            comb(n, h).start()

    def ring_end(n):
        for h in range(2):
            direct(n, h).wait()
            comb(n, h).wait()
        for jhi in range(14):
            lanes = slice(jhi * 128, (jhi + 1) * 128)
            ybuf[n, pl.ds(jhi, 16, stride=16), :] = own[n, x, :, lanes] + (fromx[n, 0, :, lanes] + fromx[n, 1, :, lanes])
        for d in range(1, 16):
            out(n, d).start()
        z_ref[n, here] = ybuf[n, here]

    def phases():
        for load in loads[3:]:
            load.wait()
        momenta = (lax.broadcasted_iota(i32, (8, 256), 1).astype(f32) + 0.5) * (momentum_top / 256)
        times = lax.broadcasted_iota(i32, (8, 256), 0).astype(f32) * time_step
        z16 = jnp.zeros((16, 256), f32)
        first = (row * 16 + ch) * 2
        for n in range(2):
            angle = energy_ref[first + n] * times + 0.5 * times * (momenta * momenta) + (phase_ref[first + n] + mp_v[...])
            cos, sin = (0.5 * time_step) * jnp.cos(angle), (0.5 * time_step) * jnp.sin(angle)
            for khi in range(2):
                c, s = cos[:, khi * 128:(khi + 1) * 128], sin[:, khi * 128:(khi + 1) * 128]
                block = jnp.concatenate([jnp.concatenate([c, s], 1), jnp.concatenate([-s, c], 1)], 0)
                hi, lo = split2(block)
                for d in range(2):
                    rows = [p for piece in (hi, hi, lo, lo) for p in ((piece, z16), (z16, piece))[d]]
                    at = (khi * 2 + d) * 256
                    fact_ref[n, :, at:at + 256] = jnp.concatenate(rows, axis=0).astype(bf16)

    def tables():
        def three(table):
            a, rest = split2(table)
            b, rest = split2(rest)
            return jnp.concatenate([a, b, rest, jnp.zeros_like(a)], axis=0).astype(bf16)

        table = jnp.concatenate([three(bv_v[...]), three(bs_v[...])], axis=1)
        level_of = lax.broadcasted_iota(i32, (128, 128), 0)
        for i in range(7):
            chosen = (level_of % 32 == jnp.broadcast_to(lev_v[i:i + 1, :], (128, 128))) & (level_of < 96)
            bt_ref[i * 128:(i + 1) * 128, :] = dot(jnp.transpose(chosen.astype(f32)).astype(bf16), table)

    def places():
        for copy in list_copies:
            copy.wait()
        row_of = jnp.transpose(lists[...])
        for i in range(7):
            channel = lax.broadcasted_iota(i32, (128, 256), 0) + i * 128
            for jlo in range(4):
                match = channel == jnp.broadcast_to(row_of[jlo * 32:jlo * 32 + 1, :], (128, 256))
                hot_ref[i * 128:(i + 1) * 128, jlo * 256:(jlo + 1) * 256] = match.astype(f32).astype(bf16)

    def split_coupling(k):
        coup_copy(k).wait()

        def some(i, _):
            at = pl.multiple_of(i * 32, 32)
            c = stage[k % 2, pl.ds(at, 32), :]
            hi = c.astype(bf16)
            to = pl.ds(pl.multiple_of(k * PART + i * 32, 32), 32)
            left_ref[to, 0:NCH] = hi
            left_ref[to, NCH:2 * NCH] = (c - hi.astype(f32)).astype(bf16)
            left_ref[to, 2 * NCH:3 * NCH] = hi
            return 0

        lax.fori_loop(0, PART // 32, some, 0)
        if k + 2 < NG // PART:
            coup_copy(k + 2).start()

    def add_fresh(n, rights):
        for d in range(1, 16):
            out(n, d).wait()
        hi, lo = split2(z_ref[n])
        picks = []
        for jlo in range(4):
            pair = [a[:, jlo * 32:(jlo + 1) * 32] for a in (hi, lo)]
            picks.append(jnp.concatenate(pair + pair, axis=1).astype(bf16))
        picks = jnp.concatenate(picks, axis=0)
        for i in range(7):
            at = pl.ds(i * 128, 128)
            chosen = dot(hot_ref[at, :], picks).astype(bf16)
            sums = dot(chosen, fact_ref[n])
            for khi in range(2):
                value_at = bt_ref[at, khi * 128:(khi + 1) * 128]
                slope_at = bt_ref[at, 256 + khi * 128:256 + (khi + 1) * 128]
                for p in range(2):
                    col = khi * 512 + p * 128
                    fresh = value_at * sums[:, col + 256:col + 384] - slope_at * sums[:, col:col + 128]
                    cols = slice((khi * 2 + p) * 128, (khi * 2 + p + 1) * 128)
                    both = slice(n * 512 + (khi * 2 + p) * 128, n * 512 + (khi * 2 + p + 1) * 128)
                    total = prev_ref[at, both] + fresh
                    amp_ref[at, both] = total
                    high = total.astype(bf16)
                    rights[at, cols] = high
                    rights[pl.ds(NCH + i * 128, 128), cols] = high
                    rights[pl.ds(2 * NCH + i * 128, 128), cols] = (total - high.astype(f32)).astype(bf16)

    for n in range(2):
        for tail in (14, 15):
            ybuf[n, pl.ds(tail, 16, stride=16), :] = jnp.zeros((16, 128), f32)
    ring_begin(0)
    for copy in list_copies:
        copy.start()
    lists[here] = listed
    add_core(0, 3)
    phases()
    split_coupling(0)
    ring_pass(0)
    ring_begin(1)
    add_core(1, 3)
    tables()
    split_coupling(1)
    ring_end(0)
    split_coupling(2)
    ring_pass(1)
    places()
    for k in range(3, 8):
        split_coupling(k)
    for copy in prev_copies:
        copy.wait()
    add_fresh(0, right_first)
    ring_end(1)
    for m in range(2):
        first_ref[m * 1024:(m + 1) * 1024, :] = dot(left_ref[m * 1024:(m + 1) * 1024, :], right_first[...])
    add_fresh(1, right_ref)


def exchange(*operands):
    dma = pltpu.SemaphoreType.DMA
    block = pltpu.VMEM((2, 4, 16, 1792), f32)
    return pl.pallas_call(
        exchange_kernel,
        out_shape=(jax.ShapeDtypeStruct((NG, 3 * NCH), bf16), jax.ShapeDtypeStruct((3 * NCH, 512), bf16),
                   jax.ShapeDtypeStruct((NG, 512), f32), jax.ShapeDtypeStruct((NCH, 1024), f32)),
        in_specs=[HBM] * 11,
        out_specs=(VM,) * 4,
        scratch_shapes=[pltpu.VMEM((1792, 128), f32), pltpu.VMEM((4, 2, 32, 128), f32), pltpu.SMEM((56,), i32),
                        pltpu.SMEM((256,), f32), pltpu.SMEM((256,), f32), pltpu.VMEM((1, 256), f32),
                        pltpu.VMEM((32, 256), f32), pltpu.VMEM((32, 256), f32), pltpu.VMEM((7, 128), i32),
                        pltpu.VMEM((2, PART, NCH), f32), block, block, block,
                        pltpu.VMEM((2, 2, 16, HALF), f32), pltpu.VMEM((2, 2, 16, 1792), f32), pltpu.VMEM((2, 256, 128), f32),
                        pltpu.VMEM((16, 128), i32), pltpu.VMEM((256, 128), i32), pltpu.VMEM((2, 256, 128), f32),
                        pltpu.VMEM((NCH, 1024), bf16), pltpu.VMEM((NCH, 512), f32), pltpu.VMEM((2, 128, 1024), bf16),
                        pltpu.VMEM((NCH, 1024), f32), pltpu.VMEM((3 * NCH, 512), bf16),
                        dma((9,)), dma((8,)), dma((2,)), dma((2, 4)), dma((2, 4)), dma((2, 2)), dma((2, 2)),
                        dma((2, 2)), dma((2, 2)), dma((2, 2)), dma((2, 2)), dma((2, 16)), dma((2, 16)), dma((16,)), dma((16,))],
        compiler_params=pltpu.CompilerParams(vmem_limit_bytes=32 * 2**20, collective_id=0, has_side_effects=True),
        cost_estimate=pl.CostEstimate(flops=3 * NG * NCH * 1024, bytes_accessed=14 * 2**20, transcendentals=0),
        name="exchange",
    )(*(pltpu.with_memory_space_constraint(a, pltpu.HBM) for a in operands))


def spread_kernel(left_ref, right_ref, first_ref, amp_ref, amp_hbm, spec_hbm, obuf, asem, fsem, osem):
    bounds = (0, 1024, 1536, 1792, 2048)

    def amp_copy(s):
        return pltpu.make_async_copy(amp_ref.at[:, pl.ds(s * 128, 128)], amp_hbm.at[:, s, :], asem.at[s])

    def first_copy(s):
        return pltpu.make_async_copy(first_ref.at[:, pl.ds(s * 128, 128)], spec_hbm.at[:, s, :], fsem.at[s])

    def out_copy(m, s):
        at = pl.ds(bounds[m], bounds[m + 1] - bounds[m])
        return pltpu.make_async_copy(obuf.at[at, pl.ds(s * 128, 128)], spec_hbm.at[at, 4 + s, :], osem.at[m, s])

    for s in range(4):
        first_copy(s).start()
    for s in range(8):
        amp_copy(s).start()
    for m in range(4):
        at = pl.ds(bounds[m], bounds[m + 1] - bounds[m])
        obuf[at, :] = dot(left_ref[at, :], right_ref[...])
        for s in range(4):
            out_copy(m, s).start()
    for s in range(4):
        first_copy(s).wait()
    for s in range(8):
        amp_copy(s).wait()
    for m in range(4):
        for s in range(4):
            out_copy(m, s).wait()


def spread(*operands):
    dma = pltpu.SemaphoreType.DMA
    return pl.pallas_call(
        spread_kernel,
        out_shape=(jax.ShapeDtypeStruct((NCH, 8, 128), f32), jax.ShapeDtypeStruct((NG, 8, 128), f32)),
        in_specs=[VM] * 4,
        out_specs=(ANY, ANY),
        scratch_shapes=[pltpu.VMEM((NG, 512), f32), dma((8,)), dma((4,)), dma((4, 4))],
        compiler_params=pltpu.CompilerParams(vmem_limit_bytes=16 * 2**20),
        cost_estimate=pl.CostEstimate(flops=3 * NG * NCH * 1024, bytes_accessed=12 * 2**20, transcendentals=0),
        name="spread",
    )(*operands)


def shards(surface_rows, he_states, energies, state_phase, momentum_phase, bessel_value, bessel_slope,
           channel_l2, surface_list, previous, coupling):
    prev = previous.reshape(NCH, 2, 2, 2, 128).transpose(0, 1, 3, 2, 4).reshape(NCH, 8, 128)
    ready = exchange(surface_rows.reshape(1792, 128), he_states.reshape(4, 2, 32, 128), surface_list, energies, state_phase,
                     momentum_phase.reshape(1, 256), bessel_value, bessel_slope, channel_l2.reshape(7, 128), prev, coupling)
    amplitudes, spectrum = spread(*ready)

    def whole(a):
        return a.reshape(-1, 2, 2, 2, 128).transpose(0, 1, 3, 2, 4).reshape(-1, 2, 2, 256)

    return whole(amplitudes), whole(spectrum)


def solution(mesh):
    split = P(None, ("row", "ch"), None, None)
    return jax.shard_map(
        shards,
        mesh=mesh,
        in_specs=(P(None, None, "ch", "row"), P(None, "row"), P(), P(), P(), P(), P(), P(), P("ch"), split, P()),
        out_specs=(split, split),
        check_vma=False,
    )
```

time: 43.8 us -> 41.5 us (0.947)
  Pallas kernels: 42.9 us -> 40.7 us
    pallas_call x1, Pallas kernels: 17.5 us -> 7.69 us  [spread(): pl.pallas_call(spread_kernel, out_shape=(jax.ShapeDtypeStruct((NCH, 8, 12...]
    pallas_call x1, Pallas kernels: 25.4 us -> 33 us  [exchange(): pl.pallas_call(exchange_kernel, out_shape=(jax.ShapeDtypeStruct((NG, 3 *...]
where the time goes in v2:
time: 41.5 us; the launch traced here: 41.3 us
  Pallas kernels  40.7 us (98%)
  between operations  0.64 us (2%)
    pallas_call x1, Pallas kernels, exchange(): pl.pallas_call(exchange_kernel, out_shape=(jax.ShapeDtypeStruct((NG, 3 *...  33 us
    pallas_call x1, Pallas kernels, spread(): pl.pallas_call(spread_kernel, out_shape=(jax.ShapeDtypeStruct((NCH, 8, 12...  7.69 us

profile of v2, /device:TPU:0, one launch (start us, length us, event | category | flops | bytes accessed | tf_op | source)
XLA Modules:
  0.0 41.3 jit_solution(418040546262320111)
XLA Ops:
  0.6 33.0 %exchange.1 = (bf16[2048,2688]{1,0:T(8,128)(2,1)S(1)}, bf16[2688,512]{1,0:T(8,128)(2,1)S(1)}, f32[2048,512]{1,0:T(8,128)S(1)}, f32[896,1024]{1,0:T(8,128)S(1)}) custom-call(f32[1792,128]{1,0:T(8,128)} %bitcast.22, f32[4,2,32,128]{3,2,1,0:T(8,128)} %bitcast.23, s32[56]{0:T(128)} %list_hbm.1, f32[256]{0:T(256)} %energy_hbm.1, f32[256]{0:T(256)} %phase_hbm.1, ...), custom_call_target="tpu_custom_call" | custom-call | flops 5637144576 | bytes 14680064 | tf_op jit(solution)/shard_map/exchange/pallas_call | solution.py:274
  33.7 7.7 %spread.1 = (f32[896,8,128]{2,1,0:T(8,128)}, f32[2048,8,128]{2,1,0:T(8,128)}) custom-call(bf16[2048,2688]{1,0:T(8,128)(2,1)S(1)} %get-tuple-element.8.left_ref, bf16[2688,512]{1,0:T(8,128)(2,1)S(1)} %get-tuple-element.9.right_ref, f32[2048,512]{1,0:T(8,128)S(1)} %get-tuple-element.10.first_ref, f32[896,1024]{1,0:T(8,128)S(1)} %get-tuple-element.11.amp_ref), custom_call_target="tpu_custom_call" | custom-call | flops 5637144576 | bytes 12582912 | tf_op jit(solution)/shard_map/spread/pallas_call | solution.py:329

commit v3 on v2

--- a/solution.py
+++ b/solution.py
@@ -10,6 +10,7 @@
 NCH, NG = 896, 2048
 HALF = 896
 PART = 256
+STEP = 448
 ANY = pl.BlockSpec(memory_space=pl.ANY)
 VM = pl.BlockSpec(memory_space=pltpu.VMEM)
 HBM = pl.BlockSpec(memory_space=pltpu.HBM)
@@ -28,7 +29,7 @@
 
 def exchange_kernel(surf_hbm, he_hbm, list_hbm, energy_hbm, phase_hbm, mp_hbm, bv_hbm, bs_hbm, lev_hbm, prev_hbm,
                     coup_hbm, left_ref, right_ref, first_ref, amp_ref,
-                    own_s, he_v, list_ref, energy_ref, phase_ref, mp_v, bv_v, bs_v, lev_v, stage, other, own, got, rel, fromx, ybuf, own_list, lists, z_ref, hot_ref, bt_ref, fact_ref,
+                    own_s, he_v, list_ref, energy_ref, phase_ref, mp_v, bv_v, bs_v, lev_v, stage, other, own, got, rel, fromx, ybuf, own_list, lists, z_ref, hot_ref, mask_ref, bt_ref, fact_ref,
                     prev_ref, right_first, load_sem, prev_sem, coup_sem, core_send, core_recv, rel_send, rel_recv,
                     dir_send, dir_recv, comb_send, comb_recv, out_send, out_recv, list_send, list_recv):
     row, ch = lax.axis_index("row"), lax.axis_index("ch")
@@ -38,9 +39,9 @@
     to_right, to_left = {"row": 2 * right + core}, {"row": 2 * left + core}
 
     loads = [pltpu.make_async_copy(src, dst, load_sem.at[k]) for k, (src, dst) in enumerate((
-        (he_hbm, he_v), (surf_hbm, own_s), (list_hbm, list_ref), (energy_hbm, energy_ref), (phase_hbm, phase_ref),
+        (surf_hbm, own_s), (he_hbm, he_v), (list_hbm, list_ref), (energy_hbm, energy_ref), (phase_hbm, phase_ref),
         (mp_hbm, mp_v), (bv_hbm, bv_v), (bs_hbm, bs_v), (lev_hbm, lev_v)))]
-    for load in loads:
+    for load in loads[:2]:
         load.start()
     barrier = pltpu.get_barrier_semaphore()
     for target in (partner, to_right, to_left):
@@ -54,7 +55,7 @@
     prev_copies = [pltpu.make_async_copy(prev_hbm.at[:, s, :], prev_ref.at[:, pl.ds(s * 128, 128)], prev_sem.at[s])
                    for s in range(8)]
 
-    loads[0].wait()
+    loads[1].wait()
     parts = []
     for side in (1 - core, core):
         for n in range(2):
@@ -63,11 +64,7 @@
     he = jnp.concatenate(parts, axis=0)
     h_hi, h_lo = split2(he)
     h_left = jnp.concatenate([h_hi, h_hi, h_lo], axis=1).astype(bf16)
-    loads[1].wait()
-    for k in range(2):
-        coup_copy(k).start()
-    for copy in prev_copies:
-        copy.start()
+    loads[0].wait()
     for jc in range(7):
         rows = jnp.concatenate([own_s[pl.ds(jc * 8 + j, 32, stride=56), :] for j in range(8)], axis=0)
         s_hi, s_lo = split2(rows)
@@ -80,24 +77,26 @@
                 other[n, xx, :, lanes] = part[at:at + 16]
                 own[n, xx, :, lanes] = part[128 + at:144 + at]
 
+    pl.semaphore_wait(barrier, 18)
+
+    def remote(src, dst, send, recv, target):
+        return pltpu.make_async_remote_copy(src_ref=src, dst_ref=dst, send_sem=send, recv_sem=recv,
+                                            device_id=target, device_id_type=MESH)
+
+    def core_copy(n, k):
+        block = (across, right, left, x)[k]
+        return remote(other.at[n, block], got.at[n, block], core_send.at[n, k], core_recv.at[n, k], partner)
+
+    for k in range(3):
+        core_copy(0, k).start()
+    for load in loads[2:]:
+        load.start()
     place = lax.broadcasted_iota(i32, (16, 128), 0) * 4 + lax.broadcasted_iota(i32, (16, 128), 1) // 32
     listed = jnp.full((16, 128), -1, i32)
     loads[2].wait()
     for j in range(56):
         listed = jnp.where(place == j, list_ref[j], listed)
     own_list[...] = listed
-    pl.semaphore_wait(barrier, 18)
-
-    def remote(src, dst, send, recv, target):
-        return pltpu.make_async_remote_copy(src_ref=src, dst_ref=dst, send_sem=send, recv_sem=recv,
-                                            device_id=target, device_id_type=MESH)
-
-    def core_copy(n, k):
-        block = (across, right, left, x)[k]
-        return remote(other.at[n, block], got.at[n, block], core_send.at[n, k], core_recv.at[n, k], partner)
-
-    for n, k in ((0, 0), (0, 1), (0, 2), (1, 0), (1, 1), (1, 2), (0, 3), (1, 3)):
-        core_copy(n, k).start()
     here = pl.ds(pl.multiple_of(ch * 16, 16), 16)
     list_copies = [remote(own_list, lists.at[here], list_send.at[d], list_recv.at[d], {"ch": (ch + d) % 16})
                    for d in range(1, 16)]
@@ -167,7 +166,7 @@
                 block = jnp.concatenate([jnp.concatenate([c, s], 1), jnp.concatenate([-s, c], 1)], 0)
                 hi, lo = split2(block)
                 for d in range(2):
-                    rows = [p for piece in (hi, hi, lo, lo) for p in ((piece, z16), (z16, piece))[d]]
+                    rows = [p for piece in (hi,) * 4 + (lo,) * 4 for p in ((piece, z16), (z16, piece))[d]]
                     at = (khi * 2 + d) * 256
                     fact_ref[n, :, at:at + 256] = jnp.concatenate(rows, axis=0).astype(bf16)
 
@@ -186,12 +185,20 @@
     def places():
         for copy in list_copies:
             copy.wait()
-        row_of = jnp.transpose(lists[...])
+        all_lists = lists[...]
+        row_of = jnp.transpose(all_lists)
+        numbers = all_lists.astype(f32)
+        wide = jnp.concatenate([numbers[:, j // 2 * 32:j // 2 * 32 + 32] for j in range(8)], axis=1)
+        number_hi, number_lo = (piece.astype(bf16) for piece in split2(wide))
         for i in range(7):
+            at = slice(i * 128, (i + 1) * 128)
             channel = lax.broadcasted_iota(i32, (128, 256), 0) + i * 128
-            for jlo in range(4):
-                match = channel == jnp.broadcast_to(row_of[jlo * 32:jlo * 32 + 1, :], (128, 256))
-                hot_ref[i * 128:(i + 1) * 128, jlo * 256:(jlo + 1) * 256] = match.astype(f32).astype(bf16)
+            match = channel == jnp.broadcast_to(row_of[0:1, :], (128, 256))
+            for jlo in range(1, 4):
+                match = match | (channel == jnp.broadcast_to(row_of[jlo * 32:jlo * 32 + 1, :], (128, 256)))
+            hot = match.astype(f32).astype(bf16)
+            hot_ref[at, :] = hot
+            mask_ref[at, :] = (dot(hot, number_hi) + dot(hot, number_lo) == channel.astype(f32)).astype(f32)
 
     def split_coupling(k):
         coup_copy(k).wait()
@@ -214,15 +221,12 @@
         for d in range(1, 16):
             out(n, d).wait()
         hi, lo = split2(z_ref[n])
-        picks = []
-        for jlo in range(4):
-            pair = [a[:, jlo * 32:(jlo + 1) * 32] for a in (hi, lo)]
-            picks.append(jnp.concatenate(pair + pair, axis=1).astype(bf16))
-        picks = jnp.concatenate(picks, axis=0)
-        for i in range(7):
-            at = pl.ds(i * 128, 128)
-            chosen = dot(hot_ref[at, :], picks).astype(bf16)
-            sums = dot(chosen, fact_ref[n])
+        picks = jnp.concatenate([a[:, jlo * 32:(jlo + 1) * 32] for jlo in range(4) for a in (hi, lo)], axis=1).astype(bf16)
+        for i in range(NCH // STEP):
+            at = pl.ds(i * STEP, STEP)
+            four = dot(hot_ref[at, :], picks) * mask_ref[at, :]
+            two = four[:, :128] + four[:, 128:]
+            sums = dot(jnp.concatenate([two, two], axis=1).astype(bf16), fact_ref[n])
             for khi in range(2):
                 value_at = bt_ref[at, khi * 128:(khi + 1) * 128]
                 slope_at = bt_ref[at, 256 + khi * 128:256 + (khi + 1) * 128]
@@ -235,16 +239,22 @@
                     amp_ref[at, both] = total
                     high = total.astype(bf16)
                     rights[at, cols] = high
-                    rights[pl.ds(NCH + i * 128, 128), cols] = high
-                    rights[pl.ds(2 * NCH + i * 128, 128), cols] = (total - high.astype(f32)).astype(bf16)
+                    rights[pl.ds(NCH + i * STEP, STEP), cols] = high
+                    rights[pl.ds(2 * NCH + i * STEP, STEP), cols] = (total - high.astype(f32)).astype(bf16)
 
     for n in range(2):
         for tail in (14, 15):
             ybuf[n, pl.ds(tail, 16, stride=16), :] = jnp.zeros((16, 128), f32)
     ring_begin(0)
+    for n, k in ((0, 3), (1, 0), (1, 1), (1, 2), (1, 3)):
+        core_copy(n, k).start()
     for copy in list_copies:
         copy.start()
     lists[here] = listed
+    for k in range(2):
+        coup_copy(k).start()
+    for copy in prev_copies:
+        copy.start()
     add_core(0, 3)
     phases()
     split_coupling(0)
@@ -283,7 +293,8 @@
                         pltpu.VMEM((2, PART, NCH), f32), block, block, block,
                         pltpu.VMEM((2, 2, 16, HALF), f32), pltpu.VMEM((2, 2, 16, 1792), f32), pltpu.VMEM((2, 256, 128), f32),
                         pltpu.VMEM((16, 128), i32), pltpu.VMEM((256, 128), i32), pltpu.VMEM((2, 256, 128), f32),
-                        pltpu.VMEM((NCH, 1024), bf16), pltpu.VMEM((NCH, 512), f32), pltpu.VMEM((2, 128, 1024), bf16),
+                        pltpu.VMEM((NCH, 256), bf16), pltpu.VMEM((NCH, 256), f32), pltpu.VMEM((NCH, 512), f32),
+                        pltpu.VMEM((2, 256, 1024), bf16),
                         pltpu.VMEM((NCH, 1024), f32), pltpu.VMEM((3 * NCH, 512), bf16),
                         dma((9,)), dma((8,)), dma((2,)), dma((2, 4)), dma((2, 4)), dma((2, 2)), dma((2, 2)),
                         dma((2, 2)), dma((2, 2)), dma((2, 2)), dma((2, 2)), dma((2, 16)), dma((2, 16)), dma((16,)), dma((16,))],

time: 41.5 us -> 40.1 us (0.966)
  Pallas kernels: 40.7 us -> 39.2 us
    pallas_call x1, Pallas kernels: 33 us -> 31.5 us  [exchange(): pl.pallas_call(exchange_kernel, out_shape=(jax.ShapeDtypeStruct((NG, 3 *...]
where the time goes in v3:
time: 40.1 us; the launch traced here: 39.8 us
  Pallas kernels  39.2 us (98%)
  between operations  0.64 us (2%)
    pallas_call x1, Pallas kernels, exchange(): pl.pallas_call(exchange_kernel, out_shape=(jax.ShapeDtypeStruct((NG, 3 *...  31.5 us
    pallas_call x1, Pallas kernels, spread(): pl.pallas_call(spread_kernel, out_shape=(jax.ShapeDtypeStruct((NCH, 8, 12...  7.69 us

profile of v3, /device:TPU:0, one launch (start us, length us, event | category | flops | bytes accessed | tf_op | source)
XLA Modules:
  0.0 39.8 jit_solution(17918001980181246908)
XLA Ops:
  0.6 31.5 %exchange.1 = (bf16[2048,2688]{1,0:T(8,128)(2,1)S(1)}, bf16[2688,512]{1,0:T(8,128)(2,1)S(1)}, f32[2048,512]{1,0:T(8,128)S(1)}, f32[896,1024]{1,0:T(8,128)S(1)}) custom-call(f32[1792,128]{1,0:T(8,128)} %bitcast.22, f32[4,2,32,128]{3,2,1,0:T(8,128)} %bitcast.23, s32[56]{0:T(128)} %list_hbm.1, f32[256]{0:T(256)} %energy_hbm.1, f32[256]{0:T(256)} %phase_hbm.1, ...), custom_call_target="tpu_custom_call" | custom-call | flops 5637144576 | bytes 14680064 | tf_op jit(solution)/shard_map/exchange/pallas_call | solution.py:284
  32.1 7.7 %spread.1 = (f32[896,8,128]{2,1,0:T(8,128)}, f32[2048,8,128]{2,1,0:T(8,128)}) custom-call(bf16[2048,2688]{1,0:T(8,128)(2,1)S(1)} %get-tuple-element.8.left_ref, bf16[2688,512]{1,0:T(8,128)(2,1)S(1)} %get-tuple-element.9.right_ref, f32[2048,512]{1,0:T(8,128)S(1)} %get-tuple-element.10.first_ref, f32[896,1024]{1,0:T(8,128)S(1)} %get-tuple-element.11.amp_ref), custom_call_target="tpu_custom_call" | custom-call | flops 5637144576 | bytes 12582912 | tf_op jit(solution)/shard_map/spread/pallas_call | solution.py:340

commit v4 on v3

--- a/solution.py
+++ b/solution.py
@@ -16,6 +16,7 @@
 HBM = pl.BlockSpec(memory_space=pltpu.HBM)
 MESH = pl.DeviceIdType.MESH
 NT = (((1,), (1,)), ((), ()))
+OFFSETS = sorted(range(1, 16), key=lambda d: -min(d // 4, 4 - d // 4) - min(d % 4, 4 - d % 4))
 
 
 def split2(x):
@@ -122,7 +123,7 @@
                       comb_recv.at[n, h], (to_right, to_left)[h])
 
     def out(n, d):
-        peer = (ch + d) % 16
+        peer = (ch // 4 + d // 4) % 4 * 4 + (ch % 4 + d % 4) % 4
         return remote(ybuf.at[n, pl.ds(pl.multiple_of(peer * 16, 16), 16)], z_ref.at[n, here],
                       out_send.at[n, d], out_recv.at[n, d], {"ch": peer})
 
@@ -147,7 +148,7 @@
         for jhi in range(14):
             lanes = slice(jhi * 128, (jhi + 1) * 128)
             ybuf[n, pl.ds(jhi, 16, stride=16), :] = own[n, x, :, lanes] + (fromx[n, 0, :, lanes] + fromx[n, 1, :, lanes])
-        for d in range(1, 16):
+        for d in OFFSETS:
             out(n, d).start()
         z_ref[n, here] = ybuf[n, here]
 

time: 40.1 us -> 40.1 us (level)
  no operation moved by 1% of the time
where the time goes in v4:
time: 40.1 us; the launch traced here: 39.8 us
  Pallas kernels  39.2 us (98%)
  between operations  0.64 us (2%)
    pallas_call x1, Pallas kernels, exchange(): pl.pallas_call(exchange_kernel, out_shape=(jax.ShapeDtypeStruct((NG, 3 *...  31.5 us
    pallas_call x1, Pallas kernels, spread(): pl.pallas_call(spread_kernel, out_shape=(jax.ShapeDtypeStruct((NCH, 8, 12...  7.69 us

profile of v4, /device:TPU:0, one launch (start us, length us, event | category | flops | bytes accessed | tf_op | source)
XLA Modules:
  0.0 39.8 jit_solution(2731469101634099885)
XLA Ops:
  0.6 31.5 %exchange.1 = (bf16[2048,2688]{1,0:T(8,128)(2,1)S(1)}, bf16[2688,512]{1,0:T(8,128)(2,1)S(1)}, f32[2048,512]{1,0:T(8,128)S(1)}, f32[896,1024]{1,0:T(8,128)S(1)}) custom-call(f32[1792,128]{1,0:T(8,128)} %bitcast.22, f32[4,2,32,128]{3,2,1,0:T(8,128)} %bitcast.23, s32[56]{0:T(128)} %list_hbm.1, f32[256]{0:T(256)} %energy_hbm.1, f32[256]{0:T(256)} %phase_hbm.1, ...), custom_call_target="tpu_custom_call" | custom-call | flops 5637144576 | bytes 14680064 | tf_op jit(solution)/shard_map/exchange/pallas_call | solution.py:285
  32.1 7.7 %spread.1 = (f32[896,8,128]{2,1,0:T(8,128)}, f32[2048,8,128]{2,1,0:T(8,128)}) custom-call(bf16[2048,2688]{1,0:T(8,128)(2,1)S(1)} %get-tuple-element.8.left_ref, bf16[2688,512]{1,0:T(8,128)(2,1)S(1)} %get-tuple-element.9.right_ref, f32[2048,512]{1,0:T(8,128)S(1)} %get-tuple-element.10.first_ref, f32[896,1024]{1,0:T(8,128)S(1)} %get-tuple-element.11.amp_ref), custom_call_target="tpu_custom_call" | custom-call | flops 5637144576 | bytes 12582912 | tf_op jit(solution)/shard_map/spread/pallas_call | solution.py:341
